TPU v7x, 32 devices: a whole 2x2x4 slice. The times are simulated.
32 devices in a mesh: section: 2 (over x), dp: 16 (over z, y, core).
Axes of the slice: x: 2, y: 2, z: 4, core: 2. Of those that a mesh axis runs over, the one named last changes fastest.
Arguments:
- embedded: bfloat16 [2, 16384, 512], P('section', 'dp'), may hold values from -6 to 6
- lengths: int32 [2, 32, 8], P('section', 'dp'), may hold values from 0 to 512, as said below
- cotangent: bfloat16 [2, 16384, 512], P('section', 'dp'), may hold values from -6 to 6
- attn_in: bfloat16 [2, 512, 1536], P('section', 'dp'), may hold values from -0.25 to 0.25
- attn_out: bfloat16 [2, 512, 512], P('section', 'dp'), may hold values from -1 to 1
- cross_weight: bfloat16 [2, 512, 1024], P('section', 'dp'), may hold values from -0.375 to 0.375
- up_weight: bfloat16 [2, 512, 2048], P('section', 'dp'), may hold values from -0.25 to 0.25
- down_weight: bfloat16 [2, 2048, 512], P('section', 'dp'), may hold values from -0.125 to 0.125
- norm_gain: float32 [2, 3, 512], P('section'), may hold values from 0.5 to 1.5
- norm_bias: float32 [2, 3, 512], P('section'), may hold values from -1.5 to 1.5
Outputs:
- result: bfloat16 [2, 16384, 512], P('section', 'dp')
- input_grads: bfloat16 [2, 16384, 512], P('section', 'dp')
- attn_in_grad: float32 [2, 512, 1536], P('section')
- attn_out_grad: float32 [2, 512, 512], P('section')
- cross_grad: float32 [2, 512, 1024], P('section')
- up_grad: float32 [2, 512, 2048], P('section')
- down_grad: float32 [2, 2048, 512], P('section')
- gain_grad: float32 [2, 3, 512], P('section')
- bias_grad: float32 [2, 3, 512], P('section')
Inputs may be any that keep to these rules, and one draw needn't show every extreme that they name: `lengths`: each row's 8 entries sum to 512. Entry j of a source row is 0 exactly when entry j of the same target row is 0, and only entries after the first can be 0.
All inputs are finite; a program needn't handle non-finite values.
Results may differ from a plain program's by a relative error of at most 0.02.
Values may be sent and summed in bfloat16 or wider, within the bound.
A program may use at most 320 MiB of HBM per device.

v0:
```python
import functools

import jax
import jax.numpy as jnp
from jax import lax
from jax.experimental import pallas as pl
from jax.experimental.pallas import tpu as pltpu
from jax.sharding import PartitionSpec as P

HEADS = 8

norm_eps = 1e-06
masked_score = -1e30
F32 = jnp.float32
BF16 = jnp.bfloat16
MESH = pl.DeviceIdType.MESH
down_columns = 256
query_scale = 0.125
LINE = 4
CALL_ROWS = 2
TILE = 512


def matmul_nn(left, right):
    return jnp.dot(left, right, preferred_element_type=F32)


def matmul_tn(left, right):
    return lax.dot_general(left, right, (((0,), (0,)), ((), ())), preferred_element_type=F32)


def matmul_nt(left, right):
    return lax.dot_general(left, right, (((1,), (1,)), ((), ())), preferred_element_type=F32)


class Steps:
    def __init__(self, body=None, items=(), stages=()):
        self.body = body
        self.items = items
        self.stages = stages
        self.count = len(items) + stages[-1][0] if items else 0
        self.next = 0

    def run(self, n):
        if n >= self.count:
            return
        for offset, act in reversed(self.stages):
            if 0 <= n - offset < len(self.items):
                item = self.items[n - offset]
                act(item)
                self.body.done.append((act, item))

    def until(self, n):
        while self.next < n:
            self.run(self.next)
            self.next += 1

    def more(self, n):
        self.until(self.next + n)

    def finish(self):
        self.until(self.count)


class Slots:
    def __init__(self, rows, ff_tiles):
        self.rows = rows
        self.count = 0
        self.qkv = self.take(3 * rows)
        self.cq = self.take(rows)
        self.kv = self.take(2 * rows)
        self.pre = self.take(ff_tiles * rows)
        self.hid = self.take(ff_tiles * rows)
        self.att = self.take(rows)
        self.oc = self.take(rows)
        self.first = self.take(rows)
        self.second = self.take(rows)
        self.mem = self.take(rows)
        self.gmem = self.take(rows)
        self.gdown = self.take(rows)
        self.gout = self.take(rows)
        self.gcross = self.take(rows)
        self.stage = self.take(rows)
        self.dout = self.take(1)
        self.xhat = self.take(3 * rows)

    def take(self, n):
        at = self.count
        self.count += n
        return at


class Body:
    def __init__(self, inner, rows, dp, ff_tiles, refs):
        self.inner = inner
        self.rows = rows
        self.ff_tiles = ff_tiles
        self.at = Slots(rows, ff_tiles)
        names = ["emb", "cot", "lengths", "gain", "bias"]
        names += ["w_in", "w_out", "w_cross", "w_up", "w_down"]
        if not inner:
            names += ["w_memory"]
        names += ["result", "grad_in", "g_in", "g_out", "g_cross", "g_up", "g_down"]
        if not inner:
            names += ["g_memory"]
        names += ["g_gain", "g_bias", "spill"]
        names += ["act", "probs", "res", "mask", "rstd", "gacc", "own_len", "src_len"]
        names += ["local_sem", "x_send", "x_recv"]
        if not inner:
            names += ["grad_sem"]
        if inner:
            names += ["wt", "wd", "x_shard", "x_grad", "r1", "r2", "r3", "gbuf", "grcv"]
            names += ["gz_s", "gz_r", "gy_s", "gy_r", "gc_s", "gc_r"]
            names += ["a1_s", "a1_r", "a2_s", "a2_r", "a3_s", "a3_r"]
            names += ["a4_s", "a4_r", "a5_s", "a5_r", "a6_s", "a6_r", "own_sem", "gs_s", "gs_r"]
        assert len(names) == len(refs), (len(names), len(refs))
        for name, ref in zip(names, refs):
            setattr(self, name, ref)
        self.sec = lax.axis_index("section")
        self.i = lax.axis_index("dp")
        self.across = (1 - self.sec, self.i)
        if inner:
            self.c = lax.rem(self.i, 2)
            self.y = lax.rem(self.i // 2, 2)
            self.z = self.i // 4
            self.core_dev = (self.sec, self.z * 4 + self.y * 2 + (1 - self.c))
            self.y_dev = (self.sec, self.z * 4 + (1 - self.y) * 2 + self.c)
            self.z_other = [lax.rem(self.z + d, LINE) for d in range(1, LINE)]
            self.z_dev = [(self.sec, zz * 4 + self.y * 2 + self.c) for zz in self.z_other]
        self.done = []
        self.draining = False
        self.encoding = True
        self.t_in = 0
        self.t_out = 3
        self.t_cross = 4
        self.t_up = 6
        self.t_down = 6 + ff_tiles
        self.t_all = 6 + 2 * ff_tiles
        self.t_mem = self.t_all
        self.w_memory_at = 6
        self.w_up_at = 8
        self.down_bands = TILE // down_columns
        self.feed_chunks = [self.w_up_at + n for n in range(ff_tiles + self.down_bands)]


    def remote(self, src, dst, send, recv, dev):
        return pltpu.make_async_remote_copy(
            src_ref=src, dst_ref=dst, send_sem=send, recv_sem=recv, device_id=dev, device_id_type=MESH
        )

    def send(self, src, dst, send, recv, dev):
        copy = self.remote(src, dst, send, recv, dev)
        if self.draining:
            copy.wait_send()
        else:
            copy.start()

    def drain(self):
        self.draining = True
        for act, item in self.done:
            act(item)
        self.draining = False
        self.done = []

    def barrier(self):
        sem = pltpu.get_barrier_semaphore()
        devs = [self.across]
        if self.inner:
            devs += [self.core_dev, self.y_dev] + self.z_dev
        for dev in devs:
            pl.semaphore_signal(sem, inc=1, device_id=dev, device_id_type=MESH)
        pl.semaphore_wait(sem, len(devs))


    def weight(self, k):
        if self.inner:
            return self.wt[k].reshape(TILE, TILE)
        if k < 3:
            return self.w_in[:, k * TILE : (k + 1) * TILE]
        if k == 3:
            return self.w_out[...]
        if k < 6:
            return self.w_cross[:, (k - 4) * TILE : (k - 3) * TILE]
        if k < 8:
            return self.w_memory[:, (k - 6) * TILE : (k - 5) * TILE]
        return self.w_up[:, (k - 8) * TILE : (k - 7) * TILE]

    def weight_up(self, t):
        if self.inner:
            return self.wt[self.w_up_at + t].reshape(TILE, TILE)
        start = t * TILE
        return self.w_up[:, pl.ds(start if isinstance(start, int) else pl.multiple_of(start, TILE), TILE)]

    def weight_down(self, t, cols=slice(None)):
        if self.inner:
            tile = self.wd[t, :, :, :, cols]
            return tile.reshape(TILE, tile.shape[-1])
        return self.w_down[t * TILE : (t + 1) * TILE, cols]

    def chunk_source(self, k):
        z, y, c = self.z, self.y, self.c
        down_at = self.w_up_at + self.ff_tiles
        if k < 3:
            src = self.w_in.at[:, pl.ds(k * TILE, TILE)]
        elif k == 3:
            src = self.w_out.at[...]
        elif k < 6:
            src = self.w_cross.at[:, pl.ds((k - 4) * TILE, TILE)]
        elif k < 8:
            src = self.x_shard.at[:, pl.ds((k - 6) * TILE, TILE)]
        elif k < down_at:
            src = self.w_up.at[:, pl.ds((k - 8) * TILE, TILE)]
        else:
            cols = pl.ds((k - down_at) * down_columns, down_columns)
            src = self.w_down.at[:, cols]
        if k < down_at:
            whole = self.wt.at[k]
            own = whole.at[z, y, c]
            line = whole.at[:, y, c]
            plane = whole.at[:, :, c]
        else:
            own = self.wd.at[z, y, c, :, cols]
            line = self.wd.at[:, y, c, :, cols]
            plane = self.wd.at[:, :, c, :, cols]
        return src, own, line, plane

    def gather1(self, k):
        src, own, line, plane = self.chunk_source(k)
        if not self.draining:
            own[...] = src[...]
        for d in range(LINE - 1):
            self.send(src, own, self.gz_s.at[k, d], self.gz_r.at[k, d], self.z_dev[d])

    def gather2(self, k):
        src, own, line, plane = self.chunk_source(k)
        for d in range(0 if self.draining else LINE - 1):
            self.remote(src, own, self.gz_s.at[k, d], self.gz_r.at[k, d], self.z_dev[d]).wait_recv()
        self.send(line, line, self.gy_s.at[k], self.gy_r.at[k], self.y_dev)

    def gather3(self, k):
        src, own, line, plane = self.chunk_source(k)
        if not self.draining:
            self.remote(line, line, self.gy_s.at[k], self.gy_r.at[k], self.y_dev).wait_recv()
        self.send(plane, plane, self.gc_s.at[k], self.gc_r.at[k], self.core_dev)

    def gather4(self, k):
        src, own, line, plane = self.chunk_source(k)
        if not self.draining:
            self.remote(plane, plane, self.gc_s.at[k], self.gc_r.at[k], self.core_dev).wait_recv()

    def gather_steps(self, chunks):
        stages = [(0, self.gather1), (2, self.gather2), (4, self.gather3), (5, self.gather4)]
        return Steps(self, chunks, stages)


    def tile_slot(self, k):
        at, rows = self.at, self.rows
        if k < 3:
            return at.qkv + k * rows
        if k == 3:
            return at.gout
        if k == 4:
            return at.cq
        if k == 5:
            return at.gcross
        if k < self.t_down:
            return at.pre + (k - self.t_up) * rows
        if k < self.t_all:
            return at.hid + (k - self.t_down) * rows
        return at.kv + (k - self.t_mem) * rows

    def whole_grad(self, k, start=0, size=TILE):
        rows = pl.ds(start, size)

        def columns(ref, n):
            return ref.at[rows, pl.ds(n * TILE, TILE)]

        if k < 3:
            return columns(self.g_in, k)
        if k == 3:
            return columns(self.g_out, 0)
        if k < 6:
            return columns(self.g_cross, k - self.t_cross)
        if k < self.t_down:
            return columns(self.g_up, k - self.t_up)
        if k < self.t_all:
            return self.g_down.at[pl.ds((k - self.t_down) * TILE + start, size), :]
        return columns(self.g_memory, k - self.t_mem)

    def from_partner(self, k):
        return self.encoding and k in (self.t_cross, self.t_cross + 1)

    def block_at(self, c, y=0, z=0):
        return c * (TILE // 2) + y * (TILE // 4) + z * (TILE // 16)

    def reduce1(self, k):
        if self.from_partner(k):
            return
        slot = self.tile_slot(k)
        half = TILE // 2
        src = self.act.at[slot, pl.ds(self.block_at(1 - self.c), half)]
        self.send(src, self.r1.at[k], self.a1_s.at[k], self.a1_r.at[k], self.core_dev)

    def reduce2(self, k):
        if self.from_partner(k):
            return
        slot = self.tile_slot(k)
        half, quarter = TILE // 2, TILE // 4
        own = pl.ds(pl.multiple_of(self.block_at(self.c), half), half)
        src = self.act.at[slot, own]
        if not self.draining:
            self.remote(
                src, self.r1.at[k], self.a1_s.at[k], self.a1_r.at[k], self.core_dev
            ).wait_recv()
            total = self.act[slot, own].astype(F32) + self.r1[k].astype(F32)
            self.act[slot, own] = total.astype(BF16)
        src = self.act.at[slot, pl.ds(self.block_at(self.c, 1 - self.y), quarter)]
        self.send(src, self.r2.at[k], self.a2_s.at[k], self.a2_r.at[k], self.y_dev)

    def reduce3(self, k):
        if self.from_partner(k):
            return
        slot = self.tile_slot(k)
        quarter, part = TILE // 4, TILE // 16
        own = pl.ds(pl.multiple_of(self.block_at(self.c, self.y), quarter), quarter)
        src = self.act.at[slot, own]
        if not self.draining:
            self.remote(
                src, self.r2.at[k], self.a2_s.at[k], self.a2_r.at[k], self.y_dev
            ).wait_recv()
            total = self.act[slot, own].astype(F32) + self.r2[k].astype(F32)
            self.act[slot, own] = total.astype(BF16)
        for d in range(LINE - 1):
            src = self.act.at[slot, pl.ds(self.block_at(self.c, self.y, self.z_other[d]), part)]
            self.send(src, self.r3.at[k, d], self.a3_s.at[k, d], self.a3_r.at[k, d], self.z_dev[d])

    def reduce4(self, k):
        if self.from_partner(k):
            return self.reduce4_memory(k)
        slot = self.tile_slot(k)
        part = TILE // 16
        own = pl.ds(pl.multiple_of(self.block_at(self.c, self.y, self.z), part), part)
        src = self.act.at[slot, own]
        if not self.draining:
            total = self.act[slot, own].astype(F32)
            for d in range(LINE - 1):
                self.remote(
                    src, self.r3.at[k, d], self.a3_s.at[k, d], self.a3_r.at[k, d], self.z_dev[d]
                ).wait_recv()
                total = total + self.r3[k, d].astype(F32)
            self.act[slot, own] = total.astype(BF16)
        if k < self.t_all:
            self.spread(k, src)
        else:
            j = k - self.t_mem
            dst = self.x_grad.at[j]
            self.send(src, dst, self.x_send.at[6 + j], self.x_recv.at[6 + j], self.across)

    def spread(self, k, src):
        part = TILE // 16
        dst = self.whole_grad(k, self.block_at(self.c, self.y, self.z), part)
        if not self.draining:
            pltpu.make_async_copy(src, dst, self.own_sem.at[k]).start()
        for d in range(LINE - 1):
            self.send(src, dst, self.a4_s.at[k, d], self.a4_r.at[k, d], self.z_dev[d])

    def reduce4_memory(self, k):
        j = k - self.t_cross
        src = self.x_grad.at[j]
        if not self.draining:
            self.remote(
                src, src, self.x_send.at[6 + j], self.x_recv.at[6 + j], self.across
            ).wait_recv()
        self.spread(k, src)

    def reduce5(self, k):
        if k >= self.t_all:
            return
        quarter, part = TILE // 4, TILE // 16
        own = self.whole_grad(k, self.block_at(self.c, self.y, self.z), part)
        if not self.draining:
            pltpu.make_async_copy(own, own, self.own_sem.at[k]).wait()
        for d in range(0 if self.draining else LINE - 1):
            self.remote(
                own, own, self.a4_s.at[k, d], self.a4_r.at[k, d], self.z_dev[d]
            ).wait_recv()
        line = self.whole_grad(k, self.block_at(self.c, self.y), quarter)
        self.send(line, line, self.a5_s.at[k], self.a5_r.at[k], self.y_dev)

    def reduce6(self, k):
        if k >= self.t_all:
            return
        half, quarter = TILE // 2, TILE // 4
        line = self.whole_grad(k, self.block_at(self.c, self.y), quarter)
        if not self.draining:
            self.remote(line, line, self.a5_s.at[k], self.a5_r.at[k], self.y_dev).wait_recv()
        plane = self.whole_grad(k, self.block_at(self.c), half)
        self.send(plane, plane, self.a6_s.at[k], self.a6_r.at[k], self.core_dev)

    def reduce7(self, k):
        if k >= self.t_all:
            return
        plane = self.whole_grad(k, self.block_at(self.c), TILE // 2)
        if not self.draining:
            self.remote(plane, plane, self.a6_s.at[k], self.a6_r.at[k], self.core_dev).wait_recv()

    def small_steps(self):
        stages = [(0, self.small1), (1, self.small2), (2, self.small3), (3, self.small4)]
        return Steps(self, [0], stages)

    def small1(self, item):
        if not self.draining:
            for j in range(6):
                self.gbuf[0, pl.ds(j, 1), :] = jnp.sum(self.gacc[j], axis=0, keepdims=True)
            self.gbuf[0, pl.ds(6, 2), :] = jnp.zeros((2, TILE), F32)
        self.send(self.gbuf.at[0], self.grcv.at[0], self.gs_s.at[0], self.gs_r.at[0], self.core_dev)

    def small2(self, item):
        if not self.draining:
            self.remote(
                self.gbuf.at[0], self.grcv.at[0], self.gs_s.at[0], self.gs_r.at[0], self.core_dev
            ).wait_recv()
            self.gbuf[1] = self.gbuf[0] + self.grcv[0]
        self.send(self.gbuf.at[1], self.grcv.at[1], self.gs_s.at[1], self.gs_r.at[1], self.y_dev)

    def small3(self, item):
        if not self.draining:
            self.remote(
                self.gbuf.at[1], self.grcv.at[1], self.gs_s.at[1], self.gs_r.at[1], self.y_dev
            ).wait_recv()
            self.gbuf[2] = self.gbuf[1] + self.grcv[1]
        for d in range(LINE - 1):
            self.send(
                self.gbuf.at[2],
                self.grcv.at[2 + self.z],
                self.gs_s.at[2 + d],
                self.gs_r.at[2 + d],
                self.z_dev[d],
            )
        if not self.draining:
            self.grcv[2 + self.z] = self.gbuf[2]

    def small4(self, item):
        if self.draining:
            return
        for d in range(LINE - 1):
            self.remote(
                self.gbuf.at[2],
                self.grcv.at[2 + self.z],
                self.gs_s.at[2 + d],
                self.gs_r.at[2 + d],
                self.z_dev[d],
            ).wait_recv()
        total = self.grcv[2]
        for n in range(1, LINE):
            total = total + self.grcv[2 + n]
        self.g_gain[...] = total[0:3]
        self.g_bias[...] = total[3:6]


    def fill_mask(self, r, key_len, causal):
        lane = lax.broadcasted_iota(jnp.int32, (8, 128), 1)
        sub = lax.broadcasted_iota(jnp.int32, (8, 128), 0)

        def ends_of(ref):
            spans = jnp.broadcast_to(ref[pl.ds(r, 1), :], (8, 128))
            return jnp.sum(jnp.where(lane <= sub, spans, 0).astype(F32), axis=1, keepdims=True)

        ends = ends_of(key_len)
        flat = jnp.sum(jnp.where(lane == sub, ends, 0.0), axis=0, keepdims=True)
        flat = jnp.where(lane[:1] < 8, flat, 1e9)
        pos = lax.broadcasted_iota(jnp.int32, (TILE, 128), 0).astype(F32)
        key_ids = jnp.sum(jnp.where(pos >= flat, 1.0, 0.0), axis=1, keepdims=True)
        query_ends = ends_of(self.own_len)
        pos = lax.broadcasted_iota(jnp.int32, (8, TILE), 1).astype(F32)
        query_ids = jnp.sum(jnp.where(pos >= query_ends, 1.0, 0.0), axis=0, keepdims=True)
        step = 128
        for b in range(TILE // step):
            allowed = key_ids[b * step : (b + 1) * step] == query_ids
            if causal:
                k_pos = lax.broadcasted_iota(jnp.int32, (step, TILE), 0) + b * step
                q_pos = lax.broadcasted_iota(jnp.int32, (step, TILE), 1)
                allowed = allowed & (k_pos <= q_pos)
            self.mask[b * step : (b + 1) * step, :] = jnp.where(allowed, 0.0, masked_score)


    def attend(self, q, k, v, out, r, first=0, count=HEADS // 2):
        act = self.act
        low = lax.broadcasted_iota(jnp.int32, (1, 128), 1) < 64

        def pair(n, carry):
            hp = first + n
            cols = pl.ds(pl.multiple_of(hp * 128, 128), 128)
            qs, ks, vs = act[q, :, cols], act[k, :, cols], act[v, :, cols]
            scores = []
            for j in range(2):
                qm = jnp.where(low if j == 0 else ~low, qs, jnp.zeros_like(qs))
                s = matmul_nt(ks, qm) + self.mask[...]
                scores.append((s, jnp.max(s, axis=0, keepdims=True)))
            weights = []
            for j, (s, top) in enumerate(scores):
                raised = jnp.exp(s - top)
                raised = raised * (1.0 / jnp.sum(raised, axis=0, keepdims=True))
                weights.append(raised.astype(BF16))
                self.probs[r, hp * 2 + j] = weights[j]
            for j, probs in enumerate(weights):
                o = matmul_tn(vs, probs)[64 * j : 64 * j + 64]
                rows = pl.ds(pl.multiple_of(hp * 128 + 64 * j, 64), 64)
                act[out, rows, :] = o.astype(BF16)
            return carry

        lax.fori_loop(0, count, pair, 0)

    def attend_back(self, q, k, v, out, dout, r, first=0, count=HEADS // 2):
        act = self.act
        low = lax.broadcasted_iota(jnp.int32, (1, 128), 1) < 64

        def pair(n, carry):
            hp = first + n
            cols = pl.ds(pl.multiple_of(hp * 128, 128), 128)
            qs, ks, vs = act[q, :, cols], act[k, :, cols], act[v, :, cols]
            grads = []
            for j in range(2):
                rows = pl.ds(pl.multiple_of(hp * 128 + 64 * j, 64), 64)
                do = act[dout, rows, :]
                prod = do.astype(F32) * act[out, rows, :].astype(F32)
                delta = jnp.sum(prod, axis=0, keepdims=True)
                none = jnp.zeros_like(do)
                do = jnp.concatenate([do, none] if j == 0 else [none, do], axis=0)
                grads.append((do, delta, matmul_nn(vs, do)))
            scores = []
            for j, (do, delta, dp) in enumerate(grads):
                probs = self.probs[r, hp * 2 + j]
                scores.append((probs, (probs.astype(F32) * (dp - delta)).astype(BF16)))
            dq, dk, dv = [], None, None
            for j, (probs, ds) in enumerate(scores):
                qm = jnp.where(low if j == 0 else ~low, qs, jnp.zeros_like(qs))
                a, b = matmul_nt(probs, grads[j][0]), matmul_nn(ds, qm)
                dv, dk = (a, b) if j == 0 else (dv + a, dk + b)
                dq.append(matmul_tn(ks, ds)[64 * j : 64 * j + 64])
            dq = (jnp.concatenate(dq, axis=0) * 0.125).astype(BF16)
            act[q, :, cols] = dq.T
            act[k, :, cols] = dk.astype(BF16)
            act[v, :, cols] = dv.astype(BF16)
            return carry

        lax.fori_loop(0, count, pair, 0)


    def blocks(self, body):
        step = 128

        def one(b, carry):
            body(pl.ds(pl.multiple_of(b * step, step), step))
            return carry

        lax.fori_loop(0, TILE // step, one, 0, unroll=True)

    def norm(self, values, n, r, rows):
        center = jnp.mean(values, axis=-1, keepdims=True)
        shifted = values - center
        scale = lax.rsqrt(jnp.mean(shifted * shifted, axis=-1, keepdims=True) + norm_eps)
        hat = shifted * scale
        self.act[self.at.xhat + n * self.rows + r, rows] = hat.astype(BF16)
        self.rstd[r, rows, pl.ds(n, 1)] = scale
        return hat * self.gain[pl.ds(n, 1), :] + self.bias[pl.ds(n, 1), :]

    def norm_back(self, grad, n, r, rows):
        hat = self.act[self.at.xhat + n * self.rows + r, rows].astype(F32)
        scale = self.rstd[r, rows, pl.ds(n, 1)]
        count = grad.shape[0] // 8
        self.gacc[n] += jnp.sum((grad * hat).reshape(count, 8, TILE), axis=0)
        self.gacc[3 + n] += jnp.sum(grad.reshape(count, 8, TILE), axis=0)
        up = grad * self.gain[pl.ds(n, 1), :]
        first = jnp.mean(up, axis=-1, keepdims=True)
        second = jnp.mean(up * hat, axis=-1, keepdims=True)
        return (up - first - hat * second) * scale


    def row(self, r):
        start = r * TILE
        return pl.ds(start if isinstance(start, int) else pl.multiple_of(start, TILE), TILE)

    def loop(self, count, body):
        def one(n, carry):
            body(n)
            return carry

        lax.fori_loop(0, count, one, 0)

    def self_in(self, r):
        x = self.emb[self.row(r), :]
        for j in range(3):
            rows = matmul_nn(x, self.weight(j))
            if j == 0:
                rows = rows * query_scale
            self.act[self.at.qkv + j * self.rows + r] = rows.astype(BF16)

    def self_forward(self, causal, steps):
        at, rows = self.at, self.rows
        base = steps.next
        steps.next += 3 * rows

        def one(r):
            self.self_in(r)
            for n in range(rows):
                pl.when(r == n)(functools.partial(steps.run, base + 3 * n))
            self.fill_mask(r, self.own_len, causal)
            q, k, v = (at.qkv + j * rows + r for j in range(3))

            def half(h):
                self.attend(q, k, v, at.att + r, r, 2 * h, 2)
                for n in range(rows):
                    for m in range(2):
                        pl.when((r == n) & (h == m))(
                            functools.partial(steps.run, base + 3 * n + 1 + m)
                        )

            self.loop(HEADS // 4, half)
            if not self.encoding:
                self.spilled(r, False).start()
            self.self_out(r)

        self.loop(rows, one)

    def self_out(self, r):
        at = self.at
        x = self.emb[self.row(r), :].astype(F32)
        self.res[r] = x + matmul_tn(self.act[at.att + r], self.weight(3))

        def block(rows):
            out = self.norm(self.res[r, rows], 0, r, rows)
            self.res[r, rows] = out
            self.act[at.first + r, rows] = out.astype(BF16)

        self.blocks(block)

    def feed_up(self, x_slot, r, t):
        at = self.at
        pre = matmul_nn(self.act[x_slot], self.weight_up(t))
        hid = (pre / (1.0 + jnp.exp(-pre))).astype(BF16)
        self.act[at.pre + t * self.rows + r] = pre.astype(BF16)
        self.act[at.hid + t * self.rows + r] = hid

    def feed_down(self, r, j):
        cols = slice(j * down_columns, (j + 1) * down_columns)
        total = self.res[r, :, cols]
        for t in range(self.ff_tiles):
            hid = self.act[self.at.hid + t * self.rows + r]
            total = total + matmul_nn(hid, self.weight_down(t, cols))
        self.res[r, :, cols] = total

    def feed_back(self, r):
        at = self.at
        grad = self.act[at.gdown + r]
        total = None
        for t in range(self.ff_tiles):
            dh = matmul_nt(grad, self.weight_down(t))
            pre = self.act[at.pre + t * self.rows + r].astype(F32)
            s = 1.0 / (1.0 + jnp.exp(-pre))
            dp = (dh * (s * (1.0 + pre * (1.0 - s)))).astype(BF16)
            self.act[at.pre + t * self.rows + r] = dp
            part = matmul_nt(dp, self.weight_up(t))
            total = part if total is None else total + part
        self.res[r] += total

    def self_back(self, r, step):
        at = self.at
        self.act[at.dout] = matmul_nt(self.weight(3), self.act[at.gout + r]).astype(BF16)
        step(0)
        q, k, v = (at.qkv + j * self.rows + r for j in range(3))

        def half(h):
            self.attend_back(q, k, v, at.att + r, at.dout, r, 2 * h, 2)
            for m in range(2):
                pl.when(h == m)(functools.partial(step, 1 + m))

        self.loop(HEADS // 4, half)
        total = self.res[r]
        for j in range(3):
            total = total + matmul_nt(self.act[at.qkv + j * self.rows + r], self.weight(j))
        self.act[at.stage + r] = total.astype(BF16)
        step(3)
        self.store(at.stage + r, self.grad_in, r, 2 + r).start()

    def both(self, slot):
        return self.act[pl.ds(slot, self.rows)].reshape(self.rows * TILE, TILE)

    def weight_grad(self, slot, left, right):
        self.act[slot] = matmul_tn(left, right).astype(BF16)

    def out_grad(self, k, left, right):
        total = matmul_nn(self.act[left], self.act[right])
        for r in range(1, self.rows):
            total = total + matmul_nn(self.act[left + r], self.act[right + r])
        self.act[self.tile_slot(k)] = total.astype(BF16)

    def down_grads(self):
        at, rows = self.at, self.rows
        grad = self.both(at.gdown)

        def part(t):
            slot = at.hid + t * rows
            self.weight_grad(slot, self.both(slot), grad)

        self.loop(self.ff_tiles, part)

    def up_grads(self, x_slot):
        at, rows = self.at, self.rows
        x = self.both(x_slot)

        def part(t):
            slot = at.pre + t * rows
            self.weight_grad(slot, x, self.both(slot))

        self.loop(self.ff_tiles, part)

    def self_grads(self):
        at = self.at
        x = self.emb[...]

        def part(j):
            slot = at.qkv + j * self.rows
            self.weight_grad(slot, x, self.both(slot))

        self.loop(3, part)
        self.out_grad(self.t_out, at.att, at.gout)


    def store(self, slot, out, r, sem):
        return pltpu.make_async_copy(
            self.act.at[slot], out.at[self.row(r), :], self.local_sem.at[sem]
        )

    def spilled(self, r, back):
        a, b = self.probs.at[r], self.spill.at[r]
        return pltpu.make_async_copy(*((b, a) if back else (a, b)), self.local_sem.at[4 + r])

    def upstream(self, slot, r):
        return pltpu.make_async_copy(
            self.cot.at[self.row(r), :], self.act.at[slot], self.local_sem.at[6 + r]
        )

    def x_copy(self, slot, r, sem):
        ref = self.act.at[slot + r]
        return self.remote(ref, ref, self.x_send.at[sem + r], self.x_recv.at[sem + r], self.across)

    def length_copy(self):
        return self.remote(
            self.own_len, self.src_len, self.x_send.at[4], self.x_recv.at[4], self.across
        )

    def shard_copy(self):
        return self.remote(
            self.w_cross, self.x_shard, self.x_send.at[5], self.x_recv.at[5], self.across
        )


    def run(self):
        self.gacc[...] = jnp.zeros(self.gacc.shape, F32)
        self.own_len[...] = jnp.zeros(self.own_len.shape, jnp.int32)
        self.own_len[pl.ds(0, self.rows), pl.ds(0, self.lengths.shape[1])] = self.lengths[...]
        self.barrier()

        @pl.when(self.sec == 0)
        def first():
            self.encoding = True
            self.encoder()

        @pl.when(self.sec == 1)
        def second():
            self.encoding = False
            self.decoder()

    def encoder(self):
        at, rows = self.at, self.rows
        self.length_copy().start()
        for r in range(rows):
            self.upstream(at.cq + r, r).start()
        steps = Steps()
        if self.inner:
            self.shard_copy().start()
            steps = self.gather_steps([0, 1, 2, 3] + self.feed_chunks)
            steps.until(9)
        self.self_forward(False, steps)
        base = max(steps.next, 10)
        steps.until(base)

        def up(t):
            for n in range(1, self.ff_tiles):
                if base <= 9 + n:
                    pl.when(t == n)(functools.partial(steps.run, 9 + n))
            for r in range(rows):
                self.feed_up(at.first + r, r, t)

        steps.next = max(base, 9 + self.ff_tiles)
        self.loop(self.ff_tiles, up)
        last = self.down_bands - 1
        for j in range(last):
            steps.until(10 + self.ff_tiles + j)
            self.loop(rows, functools.partial(self.feed_down, j=j))
        steps.finish()

        def send(r):
            self.feed_down(r, last)

            def block(b):
                second = self.norm(self.res[r, b], 1, r, b)
                self.act[at.mem + r, b] = self.norm(second, 2, r, b).astype(BF16)

            self.blocks(block)
            pl.when(r > 0)(lambda: self.x_copy(at.mem, r - 1, 0).wait_send())
            self.x_copy(at.mem, r, 0).start()
            self.store(at.mem + r, self.result, r, r).start()

        self.loop(rows, send)
        steps = Steps()
        if self.inner:
            feed = list(range(self.t_down, self.t_all)) + list(range(self.t_up, self.t_down))
            steps = self.reduce_steps(feed + [4, 5, 3, 0, 1, 2])

        def back(r):
            self.x_copy(at.gmem, r, 2).wait_recv()
            self.upstream(at.cq + r, r).wait()

            def block(b):
                up = self.act[at.cq + r, b]
                grad = up.astype(F32) + self.act[at.gmem + r, b].astype(F32)
                grad = self.norm_back(self.norm_back(grad, 2, r, b), 1, r, b)
                self.res[r, b] = grad
                self.act[at.gdown + r, b] = grad.astype(BF16)

            self.blocks(block)

            @pl.when(r == rows - 1)
            def down():
                self.down_grads()
                steps.more(3)

            self.feed_back(r)

            def block(b):
                grad = self.norm_back(self.res[r, b], 0, r, b)
                self.res[r, b] = grad
                self.act[at.gout + r, b] = grad.astype(BF16)

            self.blocks(block)

            @pl.when(r == rows - 1)
            def up():
                self.up_grads(at.first)
                steps.more(2)

            base = steps.next
            steps.next += 4

            def step(n):
                pl.when(r == rows - 1)(functools.partial(steps.run, base + n))

            self.self_back(r, step)

        self.loop(rows, back)
        small = Steps()
        if self.inner:
            small = self.small_steps()
            small.more(1)
        self.self_grads()
        small.more(1)
        steps.more(2)
        small.more(1)
        steps.finish()
        small.finish()
        self.length_copy().wait_send()
        if self.inner:
            self.shard_copy().wait_send()
            self.drain()
        self.x_copy(at.mem, rows - 1, 0).wait_send()
        for r in range(rows):
            self.store(at.mem + r, self.result, r, r).wait()
            self.store(at.stage + r, self.grad_in, r, 2 + r).wait()
        if not self.inner:
            self.keep_grads()

    def reduce_steps(self, tiles):
        stages = [(0, self.reduce1), (1, self.reduce2), (3, self.reduce3), (5, self.reduce4)]
        stages += [(7, self.reduce5), (9, self.reduce6), (10, self.reduce7)]
        return Steps(self, tiles, stages)

    def keep_grads(self):
        tiles = list(range(self.t_all))
        if self.encoding:
            tiles = [k for k in tiles if not self.from_partner(k)]
        else:
            tiles += [self.t_mem, self.t_mem + 1]
        copies = [
            pltpu.make_async_copy(
                self.act.at[self.tile_slot(k)], self.whole_grad(k), self.grad_sem.at[k]
            )
            for k in tiles
        ]
        for copy in copies:
            copy.start()
        for copy in copies:
            copy.wait()
        for j in range(3):
            self.g_gain[pl.ds(j, 1), :] = jnp.sum(self.gacc[j], axis=0, keepdims=True)
            self.g_bias[pl.ds(j, 1), :] = jnp.sum(self.gacc[3 + j], axis=0, keepdims=True)

    def decoder(self):
        at, rows = self.at, self.rows
        for r in range(rows):
            self.upstream(at.gcross + r, r).start()
        steps = Steps()
        if self.inner:
            steps = self.gather_steps(list(range(8)) + self.feed_chunks)
            self.shard_copy().wait_recv()
            steps.until(9)
        self.self_forward(True, steps)
        steps.until(13)

        def ask(r):
            queries = matmul_nn(self.act[at.first + r], self.weight(4)) * query_scale
            self.act[at.cq + r] = queries.astype(BF16)

        self.loop(rows, ask)
        self.length_copy().wait_recv()
        base = steps.next
        steps.next = steps.count

        def middle(r):
            def step(n, count):
                @pl.when(r == 0)
                def some():
                    for m in range(base + n, base + n + count):
                        steps.run(m)

            self.fill_mask(r, self.src_len, False)
            self.spilled(r, False).wait()
            self.x_copy(at.mem, r, 0).wait_recv()
            for j in range(2):
                self.act[at.kv + j * rows + r] = matmul_nn(
                    self.act[at.mem + r], self.weight(self.w_memory_at + j)
                ).astype(BF16)
            step(0, 2)
            k, v = at.kv + r, at.kv + rows + r
            self.attend(at.cq + r, k, v, at.oc + r, r)
            step(2, steps.count)
            self.res[r] += matmul_tn(self.act[at.oc + r], self.weight(5))

            def block(b):
                out = self.norm(self.res[r, b], 1, r, b)
                self.res[r, b] = out
                self.act[at.second + r, b] = out.astype(BF16)

            self.blocks(block)
            for t in range(self.ff_tiles):
                self.feed_up(at.second + r, r, t)
            for j in range(self.down_bands):
                self.feed_down(r, j)
            self.upstream(at.gcross + r, r).wait()

            def block(b):
                out = self.norm(self.res[r, b], 2, r, b)
                self.act[at.stage + r, b] = out.astype(BF16)
                up = self.act[at.gcross + r, b]
                grad = self.norm_back(up.astype(F32), 2, r, b)
                self.res[r, b] = grad
                self.act[at.gdown + r, b] = grad.astype(BF16)

            self.blocks(block)
            self.store(at.stage + r, self.result, r, r).start()
            self.feed_back(r)

            def block(b):
                grad = self.norm_back(self.res[r, b], 1, r, b)
                self.res[r, b] = grad
                self.act[at.gcross + r, b] = grad.astype(BF16)

            self.blocks(block)
            self.act[at.dout] = matmul_nt(self.weight(5), self.act[at.gcross + r]).astype(BF16)
            self.attend_back(at.cq + r, k, v, at.oc + r, at.dout, r)
            total = matmul_nt(self.act[k], self.weight(self.w_memory_at))
            total = total + matmul_nt(self.act[v], self.weight(self.w_memory_at + 1))
            self.act[at.gmem + r] = total.astype(BF16)
            self.x_copy(at.gmem, r, 2).start()
            self.spilled(r, True).start()
            self.res[r] += matmul_nt(self.act[at.cq + r], self.weight(4))

            def block(b):
                grad = self.norm_back(self.res[r, b], 0, r, b)
                self.res[r, b] = grad
                self.act[at.gout + r, b] = grad.astype(BF16)

            self.blocks(block)

        self.loop(rows, middle)
        steps, small = Steps(), Steps()
        x = self.both(at.mem)

        def memory_grad(j):
            slot = at.kv + j * rows
            self.weight_grad(slot, x, self.both(slot))

        self.loop(2, memory_grad)
        if self.inner:
            feed = list(range(self.t_down, self.t_all)) + list(range(self.t_up, self.t_down))
            steps = self.reduce_steps([self.t_mem, self.t_mem + 1] + feed + [4, 5, 3, 0, 1, 2])
            small = self.small_steps()
        steps.more(2)
        self.down_grads()
        steps.more(3)
        small.more(1)
        self.up_grads(at.second)
        steps.more(2)
        self.weight_grad(at.cq, self.both(at.first), self.both(at.cq))
        self.out_grad(self.t_cross + 1, at.oc, at.gcross)
        base = steps.next
        steps.next += 2 * rows

        def back(r):
            self.spilled(r, True).wait()
            self.store(at.stage + r, self.result, r, r).wait()

            def step(n):
                if n % 2 == 0:
                    for m in range(rows):
                        pl.when(r == m)(functools.partial(steps.run, base + 2 * m + n // 2))

            self.self_back(r, step)

        self.loop(rows, back)
        small.more(1)
        self.self_grads()
        small.more(1)
        steps.finish()
        small.finish()
        if self.inner:
            self.drain()
        for r in range(rows):
            self.x_copy(at.gmem, r, 2).wait_send()
            self.store(at.stage + r, self.grad_in, r, 2 + r).wait()
        if not self.inner:
            self.keep_grads()


def both_layers(inner, dp, call, emb, cot, lengths, gain, bias, weights):
    rows = lengths.shape[0]
    model = emb.shape[1]
    ff_tiles = weights[3].shape[1] // TILE
    tiles = 6 + 2 * ff_tiles
    sums = tiles + 2
    vmem = pl.BlockSpec(memory_space=pltpu.VMEM)
    anywhere = pl.BlockSpec(memory_space=pl.ANY)
    dma = pltpu.SemaphoreType.DMA
    square = (TILE, TILE)
    scratch = [
        pltpu.VMEM((Slots(rows, ff_tiles).count,) + square, BF16),
        pltpu.VMEM((rows, HEADS) + square, BF16),
        pltpu.VMEM((rows,) + square, F32),
        pltpu.VMEM(square, F32),
        pltpu.VMEM((rows, TILE, 128), F32),
        pltpu.VMEM((6, 8, model), F32),
        pltpu.VMEM((8, 128), jnp.int32),
        pltpu.VMEM((8, 128), jnp.int32),
        dma((8,)),
        dma((8,)),
        dma((8,)),
    ]
    if inner:
        part = TILE // 16
        chunks = 8 + ff_tiles + TILE // down_columns
        scratch += [
            pltpu.VMEM((8 + ff_tiles, LINE, 2, 2, part, TILE), BF16),
            pltpu.VMEM((LINE, 2, 2, weights[4].shape[0], TILE), BF16),
            pltpu.VMEM((part, 2 * TILE), BF16),
            pltpu.VMEM((2, part, TILE), BF16),
            pltpu.VMEM((sums, TILE // 2, TILE), BF16),
            pltpu.VMEM((sums, TILE // 4, TILE), BF16),
            pltpu.VMEM((sums, LINE - 1, part, TILE), BF16),
            pltpu.VMEM((3, 8, model), F32),
            pltpu.VMEM((2 + LINE, 8, model), F32),
        ]
        line = (LINE - 1,)
        scratch += [dma((chunks,) + line)] * 2 + [dma((chunks,))] * 4
        scratch += [dma((sums,))] * 4 + [dma((sums,) + line)] * 4
        scratch += [dma((sums,))] * 4 + [dma((sums,)), dma((2 + LINE,)), dma((2 + LINE,))]
    else:
        scratch += [dma((sums,))]

    hidden = ff_tiles * TILE
    grads = [(model, 3 * TILE), square, (model, 2 * TILE), (model, hidden), (hidden, model)]
    if not inner:
        grads += [(model, 2 * TILE)]

    def kernel(*refs):
        Body(inner, rows, dp, ff_tiles, refs).run()

    return pl.pallas_call(
        kernel,
        out_shape=(
            jax.ShapeDtypeStruct(emb.shape, BF16),
            jax.ShapeDtypeStruct(emb.shape, BF16),
            *(jax.ShapeDtypeStruct(shape, BF16) for shape in grads),
            jax.ShapeDtypeStruct(gain.shape, F32),
            jax.ShapeDtypeStruct(bias.shape, F32),
            jax.ShapeDtypeStruct((rows, HEADS) + square, BF16),
        ),
        in_specs=[vmem, anywhere] + [vmem] * (3 + len(weights)),
        out_specs=(anywhere,) * (2 + len(grads)) + (vmem, vmem, anywhere),
        scratch_shapes=scratch,
        compiler_params=pltpu.CompilerParams(
            collective_id=call, has_side_effects=True, vmem_limit_bytes=62 * 2**20
        ),
        name="layers",
    )(emb, cot, lengths, gain, bias, *weights)


def passed_along(shard, axis, by):
    count = lax.axis_size(axis)
    pairs = [(i, i + by) for i in range(count) if 0 <= i + by < count]
    return lax.ppermute(shard, axis, pairs)


def local(
    embedded,
    lengths,
    cotangent,
    attn_in,
    attn_out,
    cross_weight,
    up_weight,
    down_weight,
    norm_gain,
    norm_bias,
):
    dp = lax.axis_size("dp")
    rows = lengths.shape[1]
    shards = tuple(w[0] for w in (attn_in, attn_out, cross_weight, up_weight, down_weight))
    inner = dp == 4 * LINE and rows <= CALL_ROWS
    args = (embedded[0], cotangent[0], lengths[0], norm_gain[0], norm_bias[0])
    if inner:
        result, grad_in, *grads, gain, bias, spill = both_layers(inner, dp, 0, *args, shards)
        grads = [grad.astype(F32) for grad in grads]
    else:
        weights = tuple(lax.all_gather(w, "dp", axis=0, tiled=True) for w in shards)
        weights += (passed_along(weights[2], "section", 1),)
        parts = []
        for call in range(0, rows, CALL_ROWS):
            span = slice(call * TILE, min(rows, call + CALL_ROWS) * TILE)
            lens = args[2][call : call + CALL_ROWS]
            parts.append(
                both_layers(
                    inner, dp, call // CALL_ROWS, args[0][span], args[1][span], lens, *args[3:], weights
                )
            )
        result = jnp.concatenate([part[0] for part in parts], axis=0)
        grad_in = jnp.concatenate([part[1] for part in parts], axis=0)
        sums = [sum(part[n].astype(F32) for part in parts) for n in range(2, 10)]
        *grads, memory, gain, bias = lax.psum(tuple(sums), "dp")
        is_first = lax.axis_index("section") == 0
        grads[2] = jnp.where(is_first, passed_along(memory, "section", -1), grads[2])
    return tuple(out[None] for out in (result, grad_in, *grads, gain, bias))


def solution(mesh):
    rows = P("section", "dp", None)
    whole = P("section", None, None)
    in_specs = (rows,) * 8 + (whole,) * 2
    out_specs = (rows,) * 2 + (whole,) * 7
    return jax.shard_map(local, mesh=mesh, in_specs=in_specs, out_specs=out_specs, check_vma=False)
```

profile of v0, /device:TPU:0, one launch (start us, length us, event | category | flops | bytes accessed | tf_op | source)
XLA Modules:
  0.0 248.3 jit_solution(13001230114261561767)
XLA Ops:
  0.6 1.3 copy_bitcast_fusion
  2.0 231.5 %layers.1 = (bf16[1024,512]{1,0:T(8,128)(2,1)}, bf16[1024,512]{1,0:T(8,128)(2,1)}, bf16[512,1536]{1,0:T(8,128)(2,1)}, bf16[512,512]{1,0:T(8,128)(2,1)}, bf16[512...) custom-call(bf16[1024,512]{1,0:T(8,128)(2,1)} %bitcast.31, ...), custom_call_target="tpu_custom_call" | custom-call | tf_op jit(solution)/shard_map/layers/pallas_call | solution.py:1098
  233.5 0.0 copy-start
  233.5 4.3 %bitcast_convert_fusion = f32[1,2048,512]{2,1,0:T(8,128)} fusion(bf16[2048,512]{1,0:T(8,128)(2,1)} %get-tuple-element.24), kind=kLoop, calls=%fused_computation | loop fusion | flops 1048576 | bytes 6291456 | tf_op jit(solution)/shard_map/broadcast_in_dim | solution.py:1162
  237.8 0.0 copy-done
  237.8 0.0 copy-start.1
  237.8 2.5 %bitcast_convert_fusion.1 = f32[1,512,2048]{2,1,0:T(8,128)} fusion(bf16[512,2048]{1,0:T(8,128)(2,1)S(1)} %copy-done), kind=kLoop, calls=%fused_computation.1 | loop fusion | flops 1048576 | bytes 6291456 | tf_op jit(solution)/shard_map/broadcast_in_dim | solution.py:1162
  240.4 0.0 copy-done.1
  240.4 0.0 copy-start.2
  240.4 2.1 bitcast_convert_fusion.2
  242.5 0.0 copy-start.5
  242.5 0.0 copy-done.2
  242.5 0.0 copy-start.7
  242.5 0.0 copy-start.6
  242.5 0.0 copy-start.4
  242.5 1.6 bitcast_convert_fusion.3
  244.0 0.0 copy-start.3
  244.0 0.0 copy-done.5
  244.0 1.1 bitcast_convert_fusion.4
  245.1 0.0 copy-done.7
  245.2 0.6 copy.19
  245.8 0.0 copy-done.6
  245.8 0.6 copy.20
  246.4 0.0 copy-done.4
  246.4 1.0 copy.27
  247.3 0.0 copy-done.3
  247.3 1.0 copy.28
Async XLA Ops:
  233.5 4.4 %copy-start = (bf16[512,2048]{1,0:T(8,128)(2,1)S(1)}, bf16[512,2048]{1,0:T(8,128)(2,1)}, u32[]{:S(2)}) copy-start(bf16[512,2048]{1,0:T(8,128)(2,1)} %get-tuple-element.23) | copy-start | bytes 6291460
  237.8 2.5 %copy-start.1 = (bf16[512,1536]{1,0:T(8,128)(2,1)S(1)}, bf16[512,1536]{1,0:T(8,128)(2,1)}, u32[]{:S(2)}) copy-start(bf16[512,1536]{1,0:T(8,128)(2,1)} %get-tuple-element.20) | copy-start | bytes 4718596
  240.4 2.1 copy-start.2
  242.5 1.6 copy-start.5
  242.5 2.7 %copy-start.7 = (f32[3,512]{1,0:T(4,128)S(1)}, f32[3,512]{1,0:T(4,128)}, u32[]{:S(2)}) copy-start(f32[3,512]{1,0:T(4,128)} %get-tuple-element.25) | copy-start | bytes 18436
  242.5 3.3 %copy-start.6 = (f32[3,512]{1,0:T(4,128)S(1)}, f32[3,512]{1,0:T(4,128)}, u32[]{:S(2)}) copy-start(f32[3,512]{1,0:T(4,128)} %get-tuple-element.26) | copy-start | bytes 18436
  242.5 3.9 %copy-start.4 = (bf16[1024,512]{1,0:T(8,128)(2,1)S(1)}, bf16[1024,512]{1,0:T(8,128)(2,1)}, u32[]{:S(2)}) copy-start(bf16[1024,512]{1,0:T(8,128)(2,1)} %get-tuple-element.18) | copy-start | bytes 3145732
  244.0 3.3 %copy-start.3 = (bf16[1024,512]{1,0:T(8,128)(2,1)S(1)}, bf16[1024,512]{1,0:T(8,128)(2,1)}, u32[]{:S(2)}) copy-start(bf16[1024,512]{1,0:T(8,128)(2,1)} %get-tuple-element.19) | copy-start | bytes 3145732
where the time goes:
time: 249 us; the launch traced here: 248 us
  Pallas kernels  232 us (93%)
  other arithmetic  11.6 us (5%)
  local copies, waits for them, and re-layouts  4.49 us (2%)
    pallas_call x1, Pallas kernels, both_layers(): pl.pallas_call(kernel, out_shape=(jax.ShapeDtypeStruct(emb.shape, BF16),...  232 us
    broadcast_in_dim x5, other arithmetic, local(): return tuple((out[None] for out in (result, grad_in, *grads, gain, bias)))  11.6 us

commit v1 on v0

--- a/solution.py
+++ b/solution.py
@@ -14,7 +14,7 @@
 F32 = jnp.float32
 BF16 = jnp.bfloat16
 MESH = pl.DeviceIdType.MESH
-down_columns = 256
+down_columns = 128
 query_scale = 0.125
 LINE = 4
 CALL_ROWS = 2
@@ -96,7 +96,7 @@
         self.rows = rows
         self.ff_tiles = ff_tiles
         self.at = Slots(rows, ff_tiles)
-        names = ["emb", "cot", "lengths", "gain", "bias"]
+        names = ["emb_in", "cot", "lengths", "gain", "bias"]
         names += ["w_in", "w_out", "w_cross", "w_up", "w_down"]
         if not inner:
             names += ["w_memory"]
@@ -104,13 +104,13 @@
         if not inner:
             names += ["g_memory"]
         names += ["g_gain", "g_bias", "spill"]
-        names += ["act", "probs", "res", "mask", "rstd", "gacc", "own_len", "src_len"]
+        names += ["emb", "emb_sem", "act", "probs", "res", "mask", "rstd", "gacc", "own_len", "src_len"]
         names += ["local_sem", "x_send", "x_recv"]
         if not inner:
             names += ["grad_sem"]
         if inner:
             names += ["wt", "wd", "x_shard", "x_grad", "r1", "r2", "r3", "gbuf", "grcv"]
-            names += ["gz_s", "gz_r", "gy_s", "gy_r", "gc_s", "gc_r"]
+            names += ["gown_sem", "gz_s", "gz_r", "gy_s", "gy_r", "gc_s", "gc_r"]
             names += ["a1_s", "a1_r", "a2_s", "a2_r", "a3_s", "a3_r"]
             names += ["a4_s", "a4_r", "a5_s", "a5_r", "a6_s", "a6_r", "own_sem", "gs_s", "gs_r"]
         assert len(names) == len(refs), (len(names), len(refs))
@@ -227,12 +227,14 @@
     def gather1(self, k):
         src, own, line, plane = self.chunk_source(k)
         if not self.draining:
-            own[...] = src[...]
+            pltpu.make_async_copy(src, own, self.gown_sem.at[k]).start()
         for d in range(LINE - 1):
             self.send(src, own, self.gz_s.at[k, d], self.gz_r.at[k, d], self.z_dev[d])
 
     def gather2(self, k):
         src, own, line, plane = self.chunk_source(k)
+        if not self.draining:
+            pltpu.make_async_copy(src, own, self.gown_sem.at[k]).wait()
         for d in range(0 if self.draining else LINE - 1):
             self.remote(src, own, self.gz_s.at[k, d], self.gz_r.at[k, d], self.z_dev[d]).wait_recv()
         self.send(line, line, self.gy_s.at[k], self.gy_r.at[k], self.y_dev)
@@ -642,8 +644,8 @@
         self.act[at.pre + t * self.rows + r] = pre.astype(BF16)
         self.act[at.hid + t * self.rows + r] = hid
 
-    def feed_down(self, r, j):
-        cols = slice(j * down_columns, (j + 1) * down_columns)
+    def feed_down(self, r, j=None):
+        cols = slice(None) if j is None else slice(j * down_columns, (j + 1) * down_columns)
         total = self.res[r, :, cols]
         for t in range(self.ff_tiles):
             hid = self.act[self.at.hid + t * self.rows + r]
@@ -695,13 +697,17 @@
             total = total + matmul_nn(self.act[left + r], self.act[right + r])
         self.act[self.tile_slot(k)] = total.astype(BF16)
 
-    def down_grads(self):
+    def down_grads(self, steps):
         at, rows = self.at, self.rows
         grad = self.both(at.gdown)
+        base = steps.next
+        steps.next += self.ff_tiles
 
         def part(t):
             slot = at.hid + t * rows
             self.weight_grad(slot, self.both(slot), grad)
+            for n in range(self.ff_tiles):
+                pl.when(t == n)(functools.partial(steps.run, base + n))
 
         self.loop(self.ff_tiles, part)
 
@@ -757,10 +763,13 @@
 
 
     def run(self):
+        rows_in = pltpu.make_async_copy(self.emb_in, self.emb, self.emb_sem.at[0])
+        rows_in.start()
         self.gacc[...] = jnp.zeros(self.gacc.shape, F32)
         self.own_len[...] = jnp.zeros(self.own_len.shape, jnp.int32)
         self.own_len[pl.ds(0, self.rows), pl.ds(0, self.lengths.shape[1])] = self.lengths[...]
         self.barrier()
+        rows_in.wait()
 
         @pl.when(self.sec == 0)
         def first():
@@ -834,8 +843,7 @@
 
             @pl.when(r == rows - 1)
             def down():
-                self.down_grads()
-                steps.more(3)
+                self.down_grads(steps)
 
             self.feed_back(r)
 
@@ -849,7 +857,7 @@
             @pl.when(r == rows - 1)
             def up():
                 self.up_grads(at.first)
-                steps.more(2)
+                steps.more(1)
 
             base = steps.next
             steps.next += 4
@@ -882,8 +890,8 @@
             self.keep_grads()
 
     def reduce_steps(self, tiles):
-        stages = [(0, self.reduce1), (1, self.reduce2), (3, self.reduce3), (5, self.reduce4)]
-        stages += [(7, self.reduce5), (9, self.reduce6), (10, self.reduce7)]
+        stages = [(0, self.reduce1), (2, self.reduce2), (4, self.reduce3), (6, self.reduce4)]
+        stages += [(8, self.reduce5), (10, self.reduce6), (11, self.reduce7)]
         return Steps(self, tiles, stages)
 
     def keep_grads(self):
@@ -923,17 +931,10 @@
             self.act[at.cq + r] = queries.astype(BF16)
 
         self.loop(rows, ask)
+        steps.finish()
         self.length_copy().wait_recv()
-        base = steps.next
-        steps.next = steps.count
 
         def middle(r):
-            def step(n, count):
-                @pl.when(r == 0)
-                def some():
-                    for m in range(base + n, base + n + count):
-                        steps.run(m)
-
             self.fill_mask(r, self.src_len, False)
             self.spilled(r, False).wait()
             self.x_copy(at.mem, r, 0).wait_recv()
@@ -941,10 +942,8 @@
                 self.act[at.kv + j * rows + r] = matmul_nn(
                     self.act[at.mem + r], self.weight(self.w_memory_at + j)
                 ).astype(BF16)
-            step(0, 2)
             k, v = at.kv + r, at.kv + rows + r
             self.attend(at.cq + r, k, v, at.oc + r, r)
-            step(2, steps.count)
             self.res[r] += matmul_tn(self.act[at.oc + r], self.weight(5))
 
             def block(b):
@@ -955,8 +954,7 @@
             self.blocks(block)
             for t in range(self.ff_tiles):
                 self.feed_up(at.second + r, r, t)
-            for j in range(self.down_bands):
-                self.feed_down(r, j)
+            self.feed_down(r)
             self.upstream(at.gcross + r, r).wait()
 
             def block(b):
@@ -1007,11 +1005,10 @@
             steps = self.reduce_steps([self.t_mem, self.t_mem + 1] + feed + [4, 5, 3, 0, 1, 2])
             small = self.small_steps()
         steps.more(2)
-        self.down_grads()
-        steps.more(3)
+        self.down_grads(steps)
         small.more(1)
         self.up_grads(at.second)
-        steps.more(2)
+        steps.more(1)
         self.weight_grad(at.cq, self.both(at.first), self.both(at.cq))
         self.out_grad(self.t_cross + 1, at.oc, at.gcross)
         base = steps.next
@@ -1054,6 +1051,8 @@
     dma = pltpu.SemaphoreType.DMA
     square = (TILE, TILE)
     scratch = [
+        pltpu.VMEM(emb.shape, BF16),
+        dma((1,)),
         pltpu.VMEM((Slots(rows, ff_tiles).count,) + square, BF16),
         pltpu.VMEM((rows, HEADS) + square, BF16),
         pltpu.VMEM((rows,) + square, F32),
@@ -1081,7 +1080,7 @@
             pltpu.VMEM((2 + LINE, 8, model), F32),
         ]
         line = (LINE - 1,)
-        scratch += [dma((chunks,) + line)] * 2 + [dma((chunks,))] * 4
+        scratch += [dma((chunks,))] + [dma((chunks,) + line)] * 2 + [dma((chunks,))] * 4
         scratch += [dma((sums,))] * 4 + [dma((sums,) + line)] * 4
         scratch += [dma((sums,))] * 4 + [dma((sums,)), dma((2 + LINE,)), dma((2 + LINE,))]
     else:
@@ -1105,7 +1104,7 @@
             jax.ShapeDtypeStruct(bias.shape, F32),
             jax.ShapeDtypeStruct((rows, HEADS) + square, BF16),
         ),
-        in_specs=[vmem, anywhere] + [vmem] * (3 + len(weights)),
+        in_specs=[anywhere] * 2 + [vmem] * 3 + [anywhere if inner else vmem] * len(weights),
         out_specs=(anywhere,) * (2 + len(grads)) + (vmem, vmem, anywhere),
         scratch_shapes=scratch,
         compiler_params=pltpu.CompilerParams(

time: 249 us -> 242 us (0.972); the launches traced: 248 us -> 238 us
  Pallas kernels: 232 us -> 221 us
    pallas_call x1, Pallas kernels: 232 us -> 221 us  [both_layers(): pl.pallas_call(kernel, out_shape=(jax.ShapeDtypeStruct(emb.shape, BF16),...]
where the time goes in v1:
time: 242 us; the launch traced here: 238 us
  Pallas kernels  221 us (91%)
  other arithmetic  11.6 us (5%)
  local copies, waits for them, and re-layouts  4.49 us (2%)
    pallas_call x1, Pallas kernels, both_layers(): pl.pallas_call(kernel, out_shape=(jax.ShapeDtypeStruct(emb.shape, BF16),...  221 us
    broadcast_in_dim x5, other arithmetic, local(): return tuple((out[None] for out in (result, grad_in, *grads, gain, bias)))  11.6 us

profile of v1, /device:TPU:0, one launch (start us, length us, event | category | flops | bytes accessed | tf_op | source)
XLA Modules:
  0.0 237.6 jit_solution(17203604372150016533)
XLA Ops:
  0.6 1.3 copy_bitcast_fusion
  2.0 220.8 %layers.1 = (bf16[1024,512]{1,0:T(8,128)(2,1)}, bf16[1024,512]{1,0:T(8,128)(2,1)}, bf16[512,1536]{1,0:T(8,128)(2,1)}, bf16[512,512]{1,0:T(8,128)(2,1)}, bf16[512...) custom-call(bf16[1024,512]{1,0:T(8,128)(2,1)} %bitcast.31, ...), custom_call_target="tpu_custom_call" | custom-call | tf_op jit(solution)/shard_map/layers/pallas_call | solution.py:1097
  222.8 0.0 copy-start
  222.8 4.3 %bitcast_convert_fusion = f32[1,2048,512]{2,1,0:T(8,128)} fusion(bf16[2048,512]{1,0:T(8,128)(2,1)} %get-tuple-element.24), kind=kLoop, calls=%fused_computation | loop fusion | flops 1048576 | bytes 6291456 | tf_op jit(solution)/shard_map/broadcast_in_dim | solution.py:1161
  227.2 0.0 copy-done
  227.2 0.0 copy-start.1
  227.2 2.5 %bitcast_convert_fusion.1 = f32[1,512,2048]{2,1,0:T(8,128)} fusion(bf16[512,2048]{1,0:T(8,128)(2,1)S(1)} %copy-done), kind=kLoop, calls=%fused_computation.1 | loop fusion | flops 1048576 | bytes 6291456 | tf_op jit(solution)/shard_map/broadcast_in_dim | solution.py:1161
  229.7 0.0 copy-done.1
  229.7 0.0 copy-start.2
  229.7 2.1 bitcast_convert_fusion.2
  231.8 0.0 copy-start.5
  231.8 0.0 copy-done.2
  231.8 0.0 copy-start.7
  231.8 0.0 copy-start.6
  231.8 0.0 copy-start.4
  231.8 1.6 bitcast_convert_fusion.3
  233.4 0.0 copy-start.3
  233.4 0.0 copy-done.5
  233.4 1.1 bitcast_convert_fusion.4
  234.5 0.0 copy-done.7
  234.5 0.6 copy.19
  235.1 0.0 copy-done.6
  235.1 0.6 copy.20
  235.7 0.0 copy-done.4
  235.7 1.0 copy.27
  236.7 0.0 copy-done.3
  236.7 1.0 copy.28
Async XLA Ops:
  222.8 4.4 %copy-start = (bf16[512,2048]{1,0:T(8,128)(2,1)S(1)}, bf16[512,2048]{1,0:T(8,128)(2,1)}, u32[]{:S(2)}) copy-start(bf16[512,2048]{1,0:T(8,128)(2,1)} %get-tuple-element.23) | copy-start | bytes 6291460
  227.2 2.5 %copy-start.1 = (bf16[512,1536]{1,0:T(8,128)(2,1)S(1)}, bf16[512,1536]{1,0:T(8,128)(2,1)}, u32[]{:S(2)}) copy-start(bf16[512,1536]{1,0:T(8,128)(2,1)} %get-tuple-element.20) | copy-start | bytes 4718596
  229.7 2.1 copy-start.2
  231.8 1.6 copy-start.5
  231.8 2.7 %copy-start.7 = (f32[3,512]{1,0:T(4,128)S(1)}, f32[3,512]{1,0:T(4,128)}, u32[]{:S(2)}) copy-start(f32[3,512]{1,0:T(4,128)} %get-tuple-element.25) | copy-start | bytes 18436
  231.8 3.3 %copy-start.6 = (f32[3,512]{1,0:T(4,128)S(1)}, f32[3,512]{1,0:T(4,128)}, u32[]{:S(2)}) copy-start(f32[3,512]{1,0:T(4,128)} %get-tuple-element.26) | copy-start | bytes 18436
  231.8 3.9 %copy-start.4 = (bf16[1024,512]{1,0:T(8,128)(2,1)S(1)}, bf16[1024,512]{1,0:T(8,128)(2,1)}, u32[]{:S(2)}) copy-start(bf16[1024,512]{1,0:T(8,128)(2,1)} %get-tuple-element.18) | copy-start | bytes 3145732
  233.4 3.3 %copy-start.3 = (bf16[1024,512]{1,0:T(8,128)(2,1)S(1)}, bf16[1024,512]{1,0:T(8,128)(2,1)}, u32[]{:S(2)}) copy-start(bf16[1024,512]{1,0:T(8,128)(2,1)} %get-tuple-element.19) | copy-start | bytes 3145732

commit v2 on v1

--- a/solution.py
+++ b/solution.py
@@ -14,6 +14,7 @@
 F32 = jnp.float32
 BF16 = jnp.bfloat16
 MESH = pl.DeviceIdType.MESH
+far_count = 1
 down_columns = 128
 query_scale = 0.125
 LINE = 4
@@ -112,7 +113,9 @@
             names += ["wt", "wd", "x_shard", "x_grad", "r1", "r2", "r3", "gbuf", "grcv"]
             names += ["gown_sem", "gz_s", "gz_r", "gy_s", "gy_r", "gc_s", "gc_r"]
             names += ["a1_s", "a1_r", "a2_s", "a2_r", "a3_s", "a3_r"]
-            names += ["a4_s", "a4_r", "a5_s", "a5_r", "a6_s", "a6_r", "own_sem", "gs_s", "gs_r"]
+            names += ["away", "far", "fown_sem", "fa_s", "fa_r", "fz_s", "fz_r"]
+            names += ["fy_s", "fy_r", "fx_s", "fx_r", "a4_s", "a4_r", "a5_s", "a5_r"]
+            names += ["a6_s", "a6_r", "own_sem", "gs_s", "gs_r"]
         assert len(names) == len(refs), (len(names), len(refs))
         for name, ref in zip(names, refs):
             setattr(self, name, ref)
@@ -140,6 +143,9 @@
         self.w_memory_at = 6
         self.w_up_at = 8
         self.down_bands = TILE // down_columns
+        self.far_at = self.w_up_at + ff_tiles + self.down_bands - far_count
+        self.far_shift = far_count
+        self.far_chunks = [self.far_at + self.far_shift + n for n in range(far_count)]
         self.feed_chunks = [self.w_up_at + n for n in range(ff_tiles + self.down_bands)]
 
 
@@ -191,11 +197,10 @@
         start = t * TILE
         return self.w_up[:, pl.ds(start if isinstance(start, int) else pl.multiple_of(start, TILE), TILE)]
 
-    def weight_down(self, t, cols=slice(None)):
+    def weight_down(self, t):
         if self.inner:
-            tile = self.wd[t, :, :, :, cols]
-            return tile.reshape(TILE, tile.shape[-1])
-        return self.w_down[t * TILE : (t + 1) * TILE, cols]
+            return self.wd[t].reshape(TILE, TILE)
+        return self.w_down[t * TILE : (t + 1) * TILE, :]
 
     def chunk_source(self, k):
         z, y, c = self.z, self.y, self.c
@@ -225,6 +230,8 @@
         return src, own, line, plane
 
     def gather1(self, k):
+        if self.is_far(k):
+            return self.far1(k)
         src, own, line, plane = self.chunk_source(k)
         if not self.draining:
             pltpu.make_async_copy(src, own, self.gown_sem.at[k]).start()
@@ -232,6 +239,8 @@
             self.send(src, own, self.gz_s.at[k, d], self.gz_r.at[k, d], self.z_dev[d])
 
     def gather2(self, k):
+        if self.is_far(k):
+            return self.far2(k)
         src, own, line, plane = self.chunk_source(k)
         if not self.draining:
             pltpu.make_async_copy(src, own, self.gown_sem.at[k]).wait()
@@ -240,15 +249,65 @@
         self.send(line, line, self.gy_s.at[k], self.gy_r.at[k], self.y_dev)
 
     def gather3(self, k):
+        if self.is_far(k) and not self.encoding:
+            return self.far3(k)
         src, own, line, plane = self.chunk_source(k)
         if not self.draining:
-            self.remote(line, line, self.gy_s.at[k], self.gy_r.at[k], self.y_dev).wait_recv()
+            if self.is_far(k):
+                n = k - self.far_at
+                self.remote(plane, plane, self.fx_s.at[n], self.fx_r.at[n], self.across).wait_recv()
+            else:
+                self.remote(line, line, self.gy_s.at[k], self.gy_r.at[k], self.y_dev).wait_recv()
         self.send(plane, plane, self.gc_s.at[k], self.gc_r.at[k], self.core_dev)
 
     def gather4(self, k):
+        if self.is_far(k) and not self.encoding:
+            return
         src, own, line, plane = self.chunk_source(k)
         if not self.draining:
             self.remote(plane, plane, self.gc_s.at[k], self.gc_r.at[k], self.core_dev).wait_recv()
+
+
+    def is_far(self, k):
+        return k >= self.far_at + (0 if self.encoding else self.far_shift)
+
+    def far_copy(self, n):
+        cols = pl.ds((self.down_bands - far_count + n) * down_columns, down_columns)
+        return self.remote(
+            self.w_down.at[:, cols], self.away.at[n], self.fa_s.at[n], self.fa_r.at[n], self.across
+        )
+
+    def far1(self, k):
+        if self.encoding:
+            return
+        n = k - self.far_at - self.far_shift
+        src, own = self.away.at[n], self.far.at[n, self.z, self.y]
+        if not self.draining:
+            self.far_copy(n).wait_recv()
+            pltpu.make_async_copy(src, own, self.fown_sem.at[n]).start()
+        for d in range(LINE - 1):
+            self.send(src, own, self.fz_s.at[n, d], self.fz_r.at[n, d], self.z_dev[d])
+
+    def far2(self, k):
+        if self.encoding:
+            return
+        n = k - self.far_at - self.far_shift
+        src, own, line = self.away.at[n], self.far.at[n, self.z, self.y], self.far.at[n, :, self.y]
+        if not self.draining:
+            pltpu.make_async_copy(src, own, self.fown_sem.at[n]).wait()
+            for d in range(LINE - 1):
+                self.remote(
+                    src, own, self.fz_s.at[n, d], self.fz_r.at[n, d], self.z_dev[d]
+                ).wait_recv()
+        self.send(line, line, self.fy_s.at[n], self.fy_r.at[n], self.y_dev)
+
+    def far3(self, k):
+        n = k - self.far_at - self.far_shift
+        line = self.far.at[n, :, self.y]
+        if not self.draining:
+            self.remote(line, line, self.fy_s.at[n], self.fy_r.at[n], self.y_dev).wait_recv()
+        src, own, near, plane = self.chunk_source(self.far_at + n)
+        self.send(self.far.at[n], plane, self.fx_s.at[n], self.fx_r.at[n], self.across)
 
     def gather_steps(self, chunks):
         stages = [(0, self.gather1), (2, self.gather2), (4, self.gather3), (5, self.gather4)]
@@ -644,13 +703,12 @@
         self.act[at.pre + t * self.rows + r] = pre.astype(BF16)
         self.act[at.hid + t * self.rows + r] = hid
 
-    def feed_down(self, r, j=None):
-        cols = slice(None) if j is None else slice(j * down_columns, (j + 1) * down_columns)
-        total = self.res[r, :, cols]
+    def feed_down(self, r):
+        total = self.res[r]
         for t in range(self.ff_tiles):
             hid = self.act[self.at.hid + t * self.rows + r]
-            total = total + matmul_nn(hid, self.weight_down(t, cols))
-        self.res[r, :, cols] = total
+            total = total + matmul_nn(hid, self.weight_down(t))
+        self.res[r] = total
 
     def feed_back(self, r):
         at = self.at
@@ -789,29 +847,17 @@
         steps = Steps()
         if self.inner:
             self.shard_copy().start()
+            for n in range(far_count):
+                self.far_copy(n).start()
             steps = self.gather_steps([0, 1, 2, 3] + self.feed_chunks)
-            steps.until(9)
+            steps.until(8)
         self.self_forward(False, steps)
-        base = max(steps.next, 10)
-        steps.until(base)
-
-        def up(t):
-            for n in range(1, self.ff_tiles):
-                if base <= 9 + n:
-                    pl.when(t == n)(functools.partial(steps.run, 9 + n))
-            for r in range(rows):
+        steps.finish()
+
+        def send(r):
+            for t in range(self.ff_tiles):
                 self.feed_up(at.first + r, r, t)
-
-        steps.next = max(base, 9 + self.ff_tiles)
-        self.loop(self.ff_tiles, up)
-        last = self.down_bands - 1
-        for j in range(last):
-            steps.until(10 + self.ff_tiles + j)
-            self.loop(rows, functools.partial(self.feed_down, j=j))
-        steps.finish()
-
-        def send(r):
-            self.feed_down(r, last)
+            self.feed_down(r)
 
             def block(b):
                 second = self.norm(self.res[r, b], 1, r, b)
@@ -881,6 +927,8 @@
         self.length_copy().wait_send()
         if self.inner:
             self.shard_copy().wait_send()
+            for n in range(far_count):
+                self.far_copy(n).wait_send()
             self.drain()
         self.x_copy(at.mem, rows - 1, 0).wait_send()
         for r in range(rows):
@@ -920,21 +968,29 @@
             self.upstream(at.gcross + r, r).start()
         steps = Steps()
         if self.inner:
-            steps = self.gather_steps(list(range(8)) + self.feed_chunks)
+            steps = self.gather_steps([0, 1, 2, 3] + self.far_chunks + [4, 5, 6, 7] + self.feed_chunks)
             self.shard_copy().wait_recv()
-            steps.until(9)
+            steps.until(8)
         self.self_forward(True, steps)
-        steps.until(13)
+        steps.until(13 + far_count)
 
         def ask(r):
             queries = matmul_nn(self.act[at.first + r], self.weight(4)) * query_scale
             self.act[at.cq + r] = queries.astype(BF16)
 
         self.loop(rows, ask)
-        steps.finish()
+        steps.until(steps.count - 4)
         self.length_copy().wait_recv()
+        base = steps.next
+        steps.next = steps.count
 
         def middle(r):
+            def rest(first, last):
+                @pl.when(r == 0)
+                def some():
+                    for n in range(first, last):
+                        steps.run(n)
+
             self.fill_mask(r, self.src_len, False)
             self.spilled(r, False).wait()
             self.x_copy(at.mem, r, 0).wait_recv()
@@ -942,8 +998,10 @@
                 self.act[at.kv + j * rows + r] = matmul_nn(
                     self.act[at.mem + r], self.weight(self.w_memory_at + j)
                 ).astype(BF16)
+            rest(base, base + 2)
             k, v = at.kv + r, at.kv + rows + r
             self.attend(at.cq + r, k, v, at.oc + r, r)
+            rest(base + 2, steps.count)
             self.res[r] += matmul_tn(self.act[at.oc + r], self.weight(5))
 
             def block(b):
@@ -1081,7 +1139,14 @@
         ]
         line = (LINE - 1,)
         scratch += [dma((chunks,))] + [dma((chunks,) + line)] * 2 + [dma((chunks,))] * 4
-        scratch += [dma((sums,))] * 4 + [dma((sums,) + line)] * 4
+        scratch += [dma((sums,))] * 4 + [dma((sums,) + line)] * 2
+        shard = weights[4].shape[0]
+        scratch += [
+            pltpu.VMEM((far_count, shard, down_columns), BF16),
+            pltpu.VMEM((far_count, LINE, 2, shard, down_columns), BF16),
+        ]
+        scratch += [dma((far_count,))] * 3 + [dma((far_count,) + line)] * 2 + [dma((far_count,))] * 4
+        scratch += [dma((sums,) + line)] * 2
         scratch += [dma((sums,))] * 4 + [dma((sums,)), dma((2 + LINE,)), dma((2 + LINE,))]
     else:
         scratch += [dma((sums,))]

time: 242 us -> 238 us (0.983)
  Pallas kernels: 221 us -> 217 us
    pallas_call x1, Pallas kernels: 221 us -> 217 us  [both_layers(): pl.pallas_call(kernel, out_shape=(jax.ShapeDtypeStruct(emb.shape, BF16),...]
where the time goes in v2:
time: 238 us; the launch traced here: 234 us
  Pallas kernels  217 us (91%)
  other arithmetic  11.6 us (5%)
  local copies, waits for them, and re-layouts  4.49 us (2%)
    pallas_call x1, Pallas kernels, both_layers(): pl.pallas_call(kernel, out_shape=(jax.ShapeDtypeStruct(emb.shape, BF16),...  217 us
    broadcast_in_dim x5, other arithmetic, local(): return tuple((out[None] for out in (result, grad_in, *grads, gain, bias)))  11.6 us

profile of v2, /device:TPU:0, one launch (start us, length us, event | category | flops | bytes accessed | tf_op | source)
XLA Modules:
  0.0 233.9 jit_solution(13463819652565501752)
XLA Ops:
  0.6 1.3 copy_bitcast_fusion
  2.0 217.1 %layers.1 = (bf16[1024,512]{1,0:T(8,128)(2,1)}, bf16[1024,512]{1,0:T(8,128)(2,1)}, bf16[512,1536]{1,0:T(8,128)(2,1)}, bf16[512,512]{1,0:T(8,128)(2,1)}, bf16[512...) custom-call(bf16[1024,512]{1,0:T(8,128)(2,1)} %bitcast.31, ...), custom_call_target="tpu_custom_call" | custom-call | tf_op jit(solution)/shard_map/layers/pallas_call | solution.py:1162
  219.0 0.0 copy-start
  219.0 4.3 %bitcast_convert_fusion = f32[1,2048,512]{2,1,0:T(8,128)} fusion(bf16[2048,512]{1,0:T(8,128)(2,1)} %get-tuple-element.24), kind=kLoop, calls=%fused_computation | loop fusion | flops 1048576 | bytes 6291456 | tf_op jit(solution)/shard_map/broadcast_in_dim | solution.py:1226
  223.4 0.0 copy-done
  223.4 0.0 copy-start.1
  223.4 2.5 %bitcast_convert_fusion.1 = f32[1,512,2048]{2,1,0:T(8,128)} fusion(bf16[512,2048]{1,0:T(8,128)(2,1)S(1)} %copy-done), kind=kLoop, calls=%fused_computation.1 | loop fusion | flops 1048576 | bytes 6291456 | tf_op jit(solution)/shard_map/broadcast_in_dim | solution.py:1226
  225.9 0.0 copy-done.1
  225.9 0.0 copy-start.2
  225.9 2.1 bitcast_convert_fusion.2
  228.0 0.0 copy-start.5
  228.0 0.0 copy-done.2
  228.0 0.0 copy-start.7
  228.0 0.0 copy-start.6
  228.0 0.0 copy-start.4
  228.0 1.6 bitcast_convert_fusion.3
  229.6 0.0 copy-start.3
  229.6 0.0 copy-done.5
  229.6 1.1 bitcast_convert_fusion.4
  230.7 0.0 copy-done.7
  230.7 0.6 copy.19
  231.3 0.0 copy-done.6
  231.3 0.6 copy.20
  231.9 0.0 copy-done.4
  231.9 1.0 copy.27
  232.9 0.0 copy-done.3
  232.9 1.0 copy.28
Async XLA Ops:
  219.0 4.4 %copy-start = (bf16[512,2048]{1,0:T(8,128)(2,1)S(1)}, bf16[512,2048]{1,0:T(8,128)(2,1)}, u32[]{:S(2)}) copy-start(bf16[512,2048]{1,0:T(8,128)(2,1)} %get-tuple-element.23) | copy-start | bytes 6291460
  223.4 2.5 %copy-start.1 = (bf16[512,1536]{1,0:T(8,128)(2,1)S(1)}, bf16[512,1536]{1,0:T(8,128)(2,1)}, u32[]{:S(2)}) copy-start(bf16[512,1536]{1,0:T(8,128)(2,1)} %get-tuple-element.20) | copy-start | bytes 4718596
  225.9 2.1 copy-start.2
  228.0 1.6 copy-start.5
  228.0 2.7 %copy-start.7 = (f32[3,512]{1,0:T(4,128)S(1)}, f32[3,512]{1,0:T(4,128)}, u32[]{:S(2)}) copy-start(f32[3,512]{1,0:T(4,128)} %get-tuple-element.25) | copy-start | bytes 18436
  228.0 3.3 %copy-start.6 = (f32[3,512]{1,0:T(4,128)S(1)}, f32[3,512]{1,0:T(4,128)}, u32[]{:S(2)}) copy-start(f32[3,512]{1,0:T(4,128)} %get-tuple-element.26) | copy-start | bytes 18436
  228.0 3.9 %copy-start.4 = (bf16[1024,512]{1,0:T(8,128)(2,1)S(1)}, bf16[1024,512]{1,0:T(8,128)(2,1)}, u32[]{:S(2)}) copy-start(bf16[1024,512]{1,0:T(8,128)(2,1)} %get-tuple-element.18) | copy-start | bytes 3145732
  229.6 3.3 %copy-start.3 = (bf16[1024,512]{1,0:T(8,128)(2,1)S(1)}, bf16[1024,512]{1,0:T(8,128)(2,1)}, u32[]{:S(2)}) copy-start(bf16[1024,512]{1,0:T(8,128)(2,1)} %get-tuple-element.19) | copy-start | bytes 3145732

commit v3 on v2

--- a/solution.py
+++ b/solution.py
@@ -1040,14 +1040,6 @@
             self.act[at.gmem + r] = total.astype(BF16)
             self.x_copy(at.gmem, r, 2).start()
             self.spilled(r, True).start()
-            self.res[r] += matmul_nt(self.act[at.cq + r], self.weight(4))
-
-            def block(b):
-                grad = self.norm_back(self.res[r, b], 0, r, b)
-                self.res[r, b] = grad
-                self.act[at.gout + r, b] = grad.astype(BF16)
-
-            self.blocks(block)
 
         self.loop(rows, middle)
         steps, small = Steps(), Steps()
@@ -1064,6 +1056,18 @@
             small = self.small_steps()
         steps.more(2)
         self.down_grads(steps)
+
+        def first_norm(r):
+            self.res[r] += matmul_nt(self.act[at.cq + r], self.weight(4))
+
+            def block(b):
+                grad = self.norm_back(self.res[r, b], 0, r, b)
+                self.res[r, b] = grad
+                self.act[at.gout + r, b] = grad.astype(BF16)
+
+            self.blocks(block)
+
+        self.loop(rows, first_norm)
         small.more(1)
         self.up_grads(at.second)
         steps.more(1)

time: 238 us -> 238 us (level)
  no operation moved by 1% of the time
where the time goes in v3:
time: 238 us; the launch traced here: 233 us
  Pallas kernels  216 us (91%)
  other arithmetic  11.6 us (5%)
  local copies, waits for them, and re-layouts  4.49 us (2%)
    pallas_call x1, Pallas kernels, both_layers(): pl.pallas_call(kernel, out_shape=(jax.ShapeDtypeStruct(emb.shape, BF16),...  216 us
    broadcast_in_dim x5, other arithmetic, local(): return tuple((out[None] for out in (result, grad_in, *grads, gain, bias)))  11.6 us

profile of v3, /device:TPU:0, one launch (start us, length us, event | category | flops | bytes accessed | tf_op | source)
XLA Modules:
  0.0 233.0 jit_solution(6238354460752970356)
XLA Ops:
  0.6 1.3 copy_bitcast_fusion
  2.0 216.2 %layers.1 = (bf16[1024,512]{1,0:T(8,128)(2,1)}, bf16[1024,512]{1,0:T(8,128)(2,1)}, bf16[512,1536]{1,0:T(8,128)(2,1)}, bf16[512,512]{1,0:T(8,128)(2,1)}, bf16[512...) custom-call(bf16[1024,512]{1,0:T(8,128)(2,1)} %bitcast.31, ...), custom_call_target="tpu_custom_call" | custom-call | tf_op jit(solution)/shard_map/layers/pallas_call | solution.py:1166
  218.2 0.0 copy-start
  218.2 4.3 %bitcast_convert_fusion = f32[1,2048,512]{2,1,0:T(8,128)} fusion(bf16[2048,512]{1,0:T(8,128)(2,1)} %get-tuple-element.24), kind=kLoop, calls=%fused_computation | loop fusion | flops 1048576 | bytes 6291456 | tf_op jit(solution)/shard_map/broadcast_in_dim | solution.py:1230
  222.6 0.0 copy-done
  222.6 0.0 copy-start.1
  222.6 2.5 %bitcast_convert_fusion.1 = f32[1,512,2048]{2,1,0:T(8,128)} fusion(bf16[512,2048]{1,0:T(8,128)(2,1)S(1)} %copy-done), kind=kLoop, calls=%fused_computation.1 | loop fusion | flops 1048576 | bytes 6291456 | tf_op jit(solution)/shard_map/broadcast_in_dim | solution.py:1230
  225.1 0.0 copy-done.1
  225.1 0.0 copy-start.2
  225.1 2.1 bitcast_convert_fusion.2
  227.2 0.0 copy-start.5
  227.2 0.0 copy-done.2
  227.2 0.0 copy-start.7
  227.2 0.0 copy-start.6
  227.2 0.0 copy-start.4
  227.2 1.6 bitcast_convert_fusion.3
  228.8 0.0 copy-start.3
  228.8 0.0 copy-done.5
  228.8 1.1 bitcast_convert_fusion.4
  229.9 0.0 copy-done.7
  229.9 0.6 copy.19
  230.5 0.0 copy-done.6
  230.5 0.6 copy.20
  231.1 0.0 copy-done.4
  231.1 1.0 copy.27
  232.1 0.0 copy-done.3
  232.1 1.0 copy.28
Async XLA Ops:
  218.2 4.4 %copy-start = (bf16[512,2048]{1,0:T(8,128)(2,1)S(1)}, bf16[512,2048]{1,0:T(8,128)(2,1)}, u32[]{:S(2)}) copy-start(bf16[512,2048]{1,0:T(8,128)(2,1)} %get-tuple-element.23) | copy-start | bytes 6291460
  222.6 2.5 %copy-start.1 = (bf16[512,1536]{1,0:T(8,128)(2,1)S(1)}, bf16[512,1536]{1,0:T(8,128)(2,1)}, u32[]{:S(2)}) copy-start(bf16[512,1536]{1,0:T(8,128)(2,1)} %get-tuple-element.20) | copy-start | bytes 4718596
  225.1 2.1 copy-start.2
  227.2 1.6 copy-start.5
  227.2 2.7 %copy-start.7 = (f32[3,512]{1,0:T(4,128)S(1)}, f32[3,512]{1,0:T(4,128)}, u32[]{:S(2)}) copy-start(f32[3,512]{1,0:T(4,128)} %get-tuple-element.25) | copy-start | bytes 18436
  227.2 3.3 %copy-start.6 = (f32[3,512]{1,0:T(4,128)S(1)}, f32[3,512]{1,0:T(4,128)}, u32[]{:S(2)}) copy-start(f32[3,512]{1,0:T(4,128)} %get-tuple-element.26) | copy-start | bytes 18436
  227.2 3.9 %copy-start.4 = (bf16[1024,512]{1,0:T(8,128)(2,1)S(1)}, bf16[1024,512]{1,0:T(8,128)(2,1)}, u32[]{:S(2)}) copy-start(bf16[1024,512]{1,0:T(8,128)(2,1)} %get-tuple-element.18) | copy-start | bytes 3145732
  228.8 3.3 %copy-start.3 = (bf16[1024,512]{1,0:T(8,128)(2,1)S(1)}, bf16[1024,512]{1,0:T(8,128)(2,1)}, u32[]{:S(2)}) copy-start(bf16[1024,512]{1,0:T(8,128)(2,1)} %get-tuple-element.19) | copy-start | bytes 3145732
